TPU v7x, 32 devices: a whole 2x2x4 slice. The times are simulated.
32 devices in a mesh: orb: 8 (over y, x, core), probe: 4 (over z).
Axes of the slice: x: 2, y: 2, z: 4, core: 2. Of those that a mesh axis runs over, the one named last changes fastest.
Arguments:
- tiles: bfloat16 [32, 9, 256, 256], P('orb', None, 'probe'), may hold values from -0.0625 to 0.0625
- pattern: int32 [32, 9], P('orb'), may hold values from 0 to 1, as said below
- signs: int32 [8192, 512], P('orb', 'probe'), may hold values from 0 to 1
- previous: bfloat16 [8192, 512], P('orb', 'probe'), may hold values from -6 to 6
- current: bfloat16 [8192, 512], P('orb', 'probe'), may hold values from -6 to 6
Outputs:
- older: bfloat16 [8192, 512], P('orb', 'probe')
- newest: bfloat16 [8192, 512], P('orb', 'probe')
- moments: float32 [4, 512], P(None, 'probe')
Inputs may be any that keep to these rules, and one draw needn't show every extreme that they name: pattern[I, 4] is 1 for every row block; each row block has 4 to 9 ones; the 4 row blocks of one index of orb hold at most 28 ones together, and some index of orb holds exactly 28.
All inputs are finite; a program needn't handle non-finite values.
Results may differ from a plain program's by a relative error of at most 0.0053.
Values may be sent and summed in bfloat16 or wider, within the bound.
A program may use at most 64 MiB of HBM per device.

v0:
```python
import math
import jax
import jax.numpy as jnp
from jax import lax
from jax.sharding import PartitionSpec as P

REACH = 4
STEPS = 4


def extended(array, sides, width):
    for axis, dim in sides:
        peers, length = (lax.axis_size(axis), array.shape[dim])
        up = [(i, (i + 1) % peers) for i in range(peers)]
        down = [(j, i) for i, j in up]
        last = lax.slice_in_dim(array, length - width, length, axis=dim)
        initial = lax.slice_in_dim(array, 0, width, axis=dim)
        before = lax.ppermute(last, axis, up)
        after = lax.ppermute(initial, axis, down)
        array = jnp.concatenate([before, array, after], axis=dim)
    return array


def extend_panel(vec, block_rows):
    return extended(vec, (("orb", 0),), REACH * block_rows)


def body(tiles, pattern, signs, previous, current):
    row_blocks, offsets, shard_rows, block_rows = tiles.shape
    probe_count = previous.shape[1]
    sign_f = (2 * signs - 1).astype(jnp.float32)
    factor = 1.0 / math.sqrt(lax.axis_size("orb") * row_blocks * block_rows)
    full_tiles = lax.all_gather(tiles, "probe", axis=2, tiled=True)
    mask_b = pattern.astype(jnp.bfloat16)
    older, newest = (previous, current)
    collected = []
    for step in range(STEPS):
        blocks = extend_panel(newest, block_rows).reshape(
            row_blocks + 2 * REACH, block_rows, probe_count
        )
        windows = jnp.stack(
            [blocks[offset : offset + row_blocks] for offset in range(offsets)], axis=1
        )
        windows = windows * mask_b[:, :, None, None]
        total = jnp.einsum(
            "roij,rojp->rip", full_tiles, windows, preferred_element_type=jnp.float32
        )
        image = total.reshape(row_blocks * block_rows, probe_count)
        nxt = (2.0 * image - older.astype(jnp.float32)).astype(jnp.bfloat16)
        local_sum = jnp.sum(sign_f * nxt.astype(jnp.float32), axis=0)
        collected.append(lax.psum(local_sum, "orb") * factor)
        older, newest = (newest, nxt)
    stacked = jnp.stack(collected)
    return (older, newest, stacked)


def solution(mesh):
    placed = (
        P("orb", None, "probe", None),
        P("orb", None),
        P("orb", "probe"),
        P("orb", "probe"),
        P("orb", "probe"),
    )
    return jax.shard_map(
        body,
        mesh=mesh,
        in_specs=placed,
        out_specs=(P("orb", "probe"), P("orb", "probe"), P(None, "probe")),
        check_vma=False,
    )
```

profile of v0, /device:TPU:0, one launch (start us, length us, event | category | flops | bytes accessed | tf_op | source)
XLA Modules:
  0.0 224.4 jit_solution(14347151901448904519)
XLA Ops:
  8.4 2.9 %collective-permute-start.1 = (bf16[1024,128]{1,0:T(8,128)(2,1)}, bf16[1024,128]{1,0:T(8,128)(2,1)S(1)}, u32[]{:S(2)}, u32[]{:S(2)}) collective-permute-start(bf16[1024,128]{1,0:T(8,128)(2,1)} %param.9), channel_id=1, source_target_pairs={{4,0},{8,4},{12,8},{16,12},{20,16},{24,20},{28,24},{0,28},{5,1},{9... | collective-permute-start | bytes 786440 | tf_op jit(solution)/shard_map/ppermute | solution.py:19
  13.2 2.5 %collective-permute-done = bf16[1024,128]{1,0:T(8,128)(2,1)S(1)} collective-permute-done((bf16[1024,128]{1,0:T(8,128)(2,1)}, bf16[1024,128]{1,0:T(8,128)(2,1)S(1)}, u32[]{:S(2)}, u32[]{:S(2)}) %collective-permute-start) | collective-permute-done | bytes 262176 | tf_op jit(solution)/shard_map/ppermute | solution.py:18
  15.8 1.5 collective-permute-done.1
  25.3 76.4 %all-gather.2.cloned.1.call-done = bf16[4,9,256,256]{3,2,1,0:T(8,128)(2,1)} async-done(((bf16[4,9,64,256]{3,2,1,0:T(8,128)(2,1)}), bf16[4,9,256,256]{3,2,1,0:T(8,128)(2,1)}) %all-gather.2.cloned.1.call-update) | async-done | bytes 4718608 | tf_op jit(solution)/shard_map/all_gather | solution.py:33
  101.7 4.0 %fusion.41 = f32[4,256,128]{1,2,0:T(8,128)S(1)} fusion(bf16[4,9,256,256]{3,2,1,0:T(8,128)(2,1)} %all-gather.2.cloned.1.call-done, bf16[4,9,256,128]{2,3,1,0:T(8,128)(2,1)S(1)} %constant_dynamic-update-slice_fusion.4, bf16[4,9]{1,0:T(4,128)(2,1)S(1)} %convert_element_type.38), kind=kOutput, calls=%fused_computation.19 | convolution fusion | flops 605290496 | bytes 7602248 | tf_op jit(solution)/shard_map/roij,rojp->rip/dot_general | solution.py:45
  107.0 2.6 %collective-permute-start.3 = (bf16[1024,128]{1,0:T(8,128)(2,1)S(1)}, bf16[1024,128]{1,0:T(8,128)(2,1)S(1)}, u32[]{:S(2)}, u32[]{:S(2)}) collective-permute-start(bf16[1024,128]{1,0:T(8,128)(2,1)S(1)} %fusion.53), channel_id=1, source_target_pairs={{4,0},{8,4},{12,8},{16,12},{20,16},{24,20},{28,24},{0,28},{5,1},{9... | collective-permute-start | bytes 786440 | tf_op jit(solution)/shard_map/ppermute | solution.py:19
  110.5 4.2 %collective-permute-done.2 = bf16[1024,128]{1,0:T(8,128)(2,1)S(1)} collective-permute-done((bf16[1024,128]{1,0:T(8,128)(2,1)S(1)}, bf16[1024,128]{1,0:T(8,128)(2,1)S(1)}, u32[]{:S(2)}, u32[]{:S(2)}) %collective-permute-start.2) | collective-permute-done | bytes 262176 | tf_op jit(solution)/shard_map/ppermute | solution.py:18
  118.4 1.8 copy.56
  120.2 1.8 copy.57
  122.0 1.8 copy.59
  123.8 1.8 copy.60
  131.7 4.0 %fusion.35 = f32[4,256,128]{1,2,0:T(8,128)S(1)} fusion(bf16[4,9,256,256]{3,2,1,0:T(8,128)(2,1)} %all-gather.2.cloned.1.call-done, bf16[4,9,256,128]{2,3,1,0:T(8,128)(2,1)S(1)} %constant_dynamic-update-slice_fusion.13, bf16[4,9]{1,0:T(4,128)(2,1)S(1)} %convert_element_type.38), kind=kOutput, calls=%fused_computation.17 | convolution fusion | flops 605290496 | bytes 7602248 | tf_op jit(solution)/shard_map/roij,rojp->rip/dot_general | solution.py:45
  135.9 1.7 collective-permute-start.4
  139.6 4.7 %collective-permute-done.4 = bf16[1024,128]{1,0:T(8,128)(2,1)S(1)} collective-permute-done((bf16[1024,128]{1,0:T(8,128)(2,1)S(1)}, bf16[1024,128]{1,0:T(8,128)(2,1)S(1)}, u32[]{:S(2)}, u32[]{:S(2)}) %collective-permute-start.4) | collective-permute-done | bytes 262176 | tf_op jit(solution)/shard_map/ppermute | solution.py:18
  148.1 1.8 copy.66
  149.9 1.8 copy.67
  151.7 1.8 copy.69
  153.5 1.8 copy.70
  161.3 4.8 %fusion.29 = f32[4,256,128]{1,2,0:T(8,128)} fusion(bf16[4,9,256,256]{3,2,1,0:T(8,128)(2,1)} %all-gather.2.cloned.1.call-done, bf16[4,9,256,128]{2,3,1,0:T(8,128)(2,1)S(1)} %constant_dynamic-update-slice_fusion.22, bf16[4,9]{1,0:T(4,128)(2,1)S(1)} %convert_element_type.38), kind=kOutput, calls=%fused_computation.15 | convolution fusion | flops 605290496 | bytes 7602248 | tf_op jit(solution)/shard_map/roij,rojp->rip/dot_general | solution.py:45
  166.1 1.2 copy.73
  167.5 2.0 collective-permute-start.6
  171.0 5.2 %collective-permute-done.6 = bf16[1024,128]{1,0:T(8,128)(2,1)S(1)} collective-permute-done((bf16[1024,128]{1,0:T(8,128)(2,1)S(1)}, bf16[1024,128]{1,0:T(8,128)(2,1)S(1)}, u32[]{:S(2)}, u32[]{:S(2)}) %collective-permute-start.6) | collective-permute-done | bytes 262176 | tf_op jit(solution)/shard_map/ppermute | solution.py:18
  176.2 1.2 pad_maximum_fusion
  180.0 1.8 copy.76
  181.8 1.8 copy.77
  183.6 1.8 copy.79
  185.4 1.8 copy.80
  187.2 1.8 copy.81
  194.9 4.8 %fusion.23 = f32[4,256,128]{1,2,0:T(8,128)} fusion(bf16[4,9,256,256]{3,2,1,0:T(8,128)(2,1)} %all-gather.2.cloned.1.call-done, bf16[4,9,256,128]{2,3,1,0:T(8,128)(2,1)S(1)} %constant_dynamic-update-slice_fusion.31, bf16[4,9]{1,0:T(4,128)(2,1)S(1)} %convert_element_type.38), kind=kOutput, calls=%fused_computation.13 | convolution fusion | flops 605290496 | bytes 7602248 | tf_op jit(solution)/shard_map/roij,rojp->rip/dot_general | solution.py:45
  199.7 1.2 copy.83
  201.0 2.0 fusion.49
  203.0 13.9 %all-reduce = (f32[128]{0:T(128)S(1)}, f32[128]{0:T(128)S(1)}, f32[128]{0:T(128)S(1)}, f32[128]{0:T(128)S(1)}) all-reduce(f32[128]{0:T(128)S(1)} %get-tuple-element.4, f32[128]{0:T(128)S(1)} %get-tuple-element.5, f32[128]{0:T(128)S(1)} %get-tuple-element.6, f32[128]{0:T(128)S(1)} %get-tuple-element.3), channel_id=1, replica_groups=mesh['orb'=8,'probe'=4] {'orb'}, use_global_device_ids=true, to_apply=%region_7.0 | all-reduce | flops 512 | bytes 4096 | tf_op jit(solution)/shard_map/psum | solution.py:51
  (111 shorter events, 45.4 us)
Async XLA Ops:
  7.2 8.6 %copy-start.1 = (bf16[1024,128]{1,0:T(8,128)(2,1)S(1)}, bf16[1024,128]{1,0:T(8,128)(2,1)}, u32[]{:S(2)}) copy-start(bf16[1024,128]{1,0:T(8,128)(2,1)} %param.9) | copy-start | bytes 786436
  7.2 94.5 %all-gather.2.cloned.1.call-start = ((), (), s32[]{:S(2)}) async-start(), calls=%async_computation | async-start | bytes 5898240 | tf_op jit(solution)/shard_map/all_gather | solution.py:33
  7.9 7.8 %collective-permute-start = (bf16[1024,128]{1,0:T(8,128)(2,1)}, bf16[1024,128]{1,0:T(8,128)(2,1)S(1)}, u32[]{:S(2)}, u32[]{:S(2)}) collective-permute-start(bf16[1024,128]{1,0:T(8,128)(2,1)} %param.9), channel_id=1, source_target_pairs={{0,4},{4,8},{8,12},{12,16},{16,20},{20,24},{24,28},{28,0},{1,5},{5... | collective-permute-start | bytes 786440 | tf_op jit(solution)/shard_map/ppermute | solution.py:18
  8.4 8.9 %collective-permute-start.1 = (bf16[1024,128]{1,0:T(8,128)(2,1)}, bf16[1024,128]{1,0:T(8,128)(2,1)S(1)}, u32[]{:S(2)}, u32[]{:S(2)}) collective-permute-start(bf16[1024,128]{1,0:T(8,128)(2,1)} %param.9), channel_id=1, source_target_pairs={{4,0},{8,4},{12,8},{16,12},{20,16},{24,20},{28,24},{0,28},{5,1},{9... | collective-permute-start | bytes 786440 | tf_op jit(solution)/shard_map/ppermute | solution.py:19
  23.0 2.1 copy-start.5
  23.0 2.2 copy-start.3
  23.0 2.2 copy-start.4
  23.0 2.2 copy-start.2
  107.0 7.7 %collective-permute-start.2 = (bf16[1024,128]{1,0:T(8,128)(2,1)S(1)}, bf16[1024,128]{1,0:T(8,128)(2,1)S(1)}, u32[]{:S(2)}, u32[]{:S(2)}) collective-permute-start(bf16[1024,128]{1,0:T(8,128)(2,1)S(1)} %fusion.53), channel_id=1, source_target_pairs={{0,4},{4,8},{8,12},{12,16},{16,20},{20,24},{24,28},{28,0},{1,5},{5... | collective-permute-start | bytes 786440 | tf_op jit(solution)/shard_map/ppermute | solution.py:18
  107.0 7.7 %collective-permute-start.3 = (bf16[1024,128]{1,0:T(8,128)(2,1)S(1)}, bf16[1024,128]{1,0:T(8,128)(2,1)S(1)}, u32[]{:S(2)}, u32[]{:S(2)}) collective-permute-start(bf16[1024,128]{1,0:T(8,128)(2,1)S(1)} %fusion.53), channel_id=1, source_target_pairs={{4,0},{8,4},{12,8},{16,12},{20,16},{24,20},{28,24},{0,28},{5,1},{9... | collective-permute-start | bytes 786440 | tf_op jit(solution)/shard_map/ppermute | solution.py:19
  126.6 4.9 %copy-start.7 = (bf16[4,1,256,128]{2,3,1,0:T(8,128)(2,1)S(1)}, bf16[4,1,256,128]{2,3,1,0:T(8,128)(2,1)}, u32[]{:S(2)}) copy-start(bf16[4,1,256,128]{2,3,1,0:T(8,128)(2,1)} %copy.60) | copy-start | bytes 786436
  126.6 5.0 %copy-start.8 = (bf16[4,1,256,128]{2,3,1,0:T(8,128)(2,1)S(1)}, bf16[4,1,256,128]{2,3,1,0:T(8,128)(2,1)}, u32[]{:S(2)}) copy-start(bf16[4,1,256,128]{2,3,1,0:T(8,128)(2,1)} %copy.61) | copy-start | bytes 786436
  135.9 8.4 %collective-permute-start.4 = (bf16[1024,128]{1,0:T(8,128)(2,1)S(1)}, bf16[1024,128]{1,0:T(8,128)(2,1)S(1)}, u32[]{:S(2)}, u32[]{:S(2)}) collective-permute-start(bf16[1024,128]{1,0:T(8,128)(2,1)S(1)} %fusion.52), channel_id=1, source_target_pairs={{0,4},{4,8},{8,12},{12,16},{16,20},{20,24},{24,28},{28,0},{1,5},{5... | collective-permute-start | bytes 786440 | tf_op jit(solution)/shard_map/ppermute | solution.py:18
  137.7 6.7 %collective-permute-start.5 = (bf16[1024,128]{1,0:T(8,128)(2,1)S(1)}, bf16[1024,128]{1,0:T(8,128)(2,1)S(1)}, u32[]{:S(2)}, u32[]{:S(2)}) collective-permute-start(bf16[1024,128]{1,0:T(8,128)(2,1)S(1)} %fusion.52), channel_id=1, source_target_pairs={{4,0},{8,4},{12,8},{16,12},{20,16},{24,20},{28,24},{0,28},{5,1},{9... | collective-permute-start | bytes 786440 | tf_op jit(solution)/shard_map/ppermute | solution.py:19
  156.3 4.9 %copy-start.9 = (bf16[4,1,256,128]{2,3,1,0:T(8,128)(2,1)S(1)}, bf16[4,1,256,128]{2,3,1,0:T(8,128)(2,1)}, u32[]{:S(2)}) copy-start(bf16[4,1,256,128]{2,3,1,0:T(8,128)(2,1)} %copy.70) | copy-start | bytes 786436
  156.3 5.0 %copy-start.10 = (bf16[4,1,256,128]{2,3,1,0:T(8,128)(2,1)S(1)}, bf16[4,1,256,128]{2,3,1,0:T(8,128)(2,1)}, u32[]{:S(2)}) copy-start(bf16[4,1,256,128]{2,3,1,0:T(8,128)(2,1)} %copy.71) | copy-start | bytes 786436
  167.4 33.5 %copy-start = (bf16[1024,128]{1,0:T(8,128)(2,1)}, bf16[1024,128]{1,0:T(8,128)(2,1)S(1)}, u32[]{:S(2)}) copy-start(bf16[1024,128]{1,0:T(8,128)(2,1)S(1)} %fusion.48) | copy-start | bytes 786436
  167.5 8.7 %collective-permute-start.6 = (bf16[1024,128]{1,0:T(8,128)(2,1)S(1)}, bf16[1024,128]{1,0:T(8,128)(2,1)S(1)}, u32[]{:S(2)}, u32[]{:S(2)}) collective-permute-start(bf16[1024,128]{1,0:T(8,128)(2,1)S(1)} %fusion.48), channel_id=1, source_target_pairs={{0,4},{4,8},{8,12},{12,16},{16,20},{20,24},{24,28},{28,0},{1,5},{5... | collective-permute-start | bytes 786440 | tf_op jit(solution)/shard_map/ppermute | solution.py:18
  169.5 6.7 %collective-permute-start.7 = (bf16[1024,128]{1,0:T(8,128)(2,1)S(1)}, bf16[1024,128]{1,0:T(8,128)(2,1)S(1)}, u32[]{:S(2)}, u32[]{:S(2)}) collective-permute-start(bf16[1024,128]{1,0:T(8,128)(2,1)S(1)} %fusion.48), channel_id=1, source_target_pairs={{4,0},{8,4},{12,8},{16,12},{20,16},{24,20},{28,24},{0,28},{5,1},{9... | collective-permute-start | bytes 786440 | tf_op jit(solution)/shard_map/ppermute | solution.py:19
  189.9 4.9 %copy-start.11 = (bf16[4,1,256,128]{2,3,1,0:T(8,128)(2,1)S(1)}, bf16[4,1,256,128]{2,3,1,0:T(8,128)(2,1)}, u32[]{:S(2)}) copy-start(bf16[4,1,256,128]{2,3,1,0:T(8,128)(2,1)} %copy.80) | copy-start | bytes 786436
  189.9 5.0 %copy-start.12 = (bf16[4,1,256,128]{2,3,1,0:T(8,128)(2,1)S(1)}, bf16[4,1,256,128]{2,3,1,0:T(8,128)(2,1)}, u32[]{:S(2)}) copy-start(bf16[4,1,256,128]{2,3,1,0:T(8,128)(2,1)} %copy.81) | copy-start | bytes 786436
  189.9 5.0 %copy-start.6 = (bf16[4,1,256,128]{2,3,1,0:T(8,128)(2,1)S(1)}, bf16[4,1,256,128]{2,3,1,0:T(8,128)(2,1)}, u32[]{:S(2)}) copy-start(bf16[4,1,256,128]{2,3,1,0:T(8,128)(2,1)} %copy.82) | copy-start | bytes 786436
Sparse Core Ops, SparseCore 0:
  9.6 92.0 all-gather.1
where the time goes:
time: 226 us; the launch traced here: 224 us
  waiting for transfers between devices  95.2 us (42%)
  local copies, waits for them, and re-layouts  63.6 us (28%)
  matrix products  17.6 us (8%)
  between operations  14.6 us (6%)
  blocking collectives  13.9 us (6%)
  starting transfers between devices  11.7 us (5%)
  other arithmetic  7.73 us (3%)
    all_gather x1, waiting for transfers between devices, body(): full_tiles = lax.all_gather(tiles, 'probe', axis=2, tiled=True)  76.4 us
    another operation x40, local copies, waits for them, and re-layouts, body(): jnp.stack([blocks[offset:offset + row_blocks] for offset in range(offsets...  40.6 us
    unnamed x60, local copies, waits for them, and re-layouts  20 us
    dot_general x4, matrix products, body(): jnp.einsum('roij,rojp->rip', full_tiles, windows, preferred_element_type=...  17.6 us
    ppermute x4, waiting for transfers between devices, extended(): before = lax.ppermute(last, axis, up)  16.6 us
    psum x1, blocking collectives, body(): collected.append(lax.psum(local_sum, 'orb') * factor)  13.9 us
    ppermute x4, starting transfers between devices, extended(): after = lax.ppermute(initial, axis, down)  7.37 us
  transfers between devices with their start and end apart: 9, of which 6 were waited for; matrix products, arithmetic and copies ran while one was open for 5% of the time, Pallas kernels for 0%

commit v1 on v0

--- a/solution.py
+++ b/solution.py
@@ -48,7 +48,7 @@
         image = total.reshape(row_blocks * block_rows, probe_count)
         nxt = (2.0 * image - older.astype(jnp.float32)).astype(jnp.bfloat16)
         local_sum = jnp.sum(sign_f * nxt.astype(jnp.float32), axis=0)
-        collected.append(lax.psum(local_sum, "orb") * factor)
+        collected.append(jnp.sum(lax.all_gather(local_sum, "orb"), axis=0) * factor)
         older, newest = (newest, nxt)
     stacked = jnp.stack(collected)
     return (older, newest, stacked)

time: 226 us -> 247 us (1.093)
  blocking collectives: 13.9 us -> 35.1 us
    all_gather x0 -> x4, blocking collectives: none -> 35.1 us  [body(): collected.append(jnp.sum(lax.all_gather(local_sum, 'orb'), axis=0) * factor)]
    psum x1 -> x0, blocking collectives: 13.9 us -> none  [body(): collected.append(lax.psum(local_sum, 'orb') * factor)]
where the time goes in v1:
time: 247 us; the launch traced here: 245 us
  waiting for transfers between devices  95.2 us (39%)
  local copies, waits for them, and re-layouts  63.4 us (26%)
  blocking collectives  35.1 us (14%)
  matrix products  17.6 us (7%)
  between operations  14.5 us (6%)
  starting transfers between devices  11.7 us (5%)
  other arithmetic  7.78 us (3%)
    all_gather x1, waiting for transfers between devices, body(): full_tiles = lax.all_gather(tiles, 'probe', axis=2, tiled=True)  76.5 us
    another operation x40, local copies, waits for them, and re-layouts, body(): jnp.stack([blocks[offset:offset + row_blocks] for offset in range(offsets...  40.4 us
    all_gather x4, blocking collectives, body(): collected.append(jnp.sum(lax.all_gather(local_sum, 'orb'), axis=0) * factor)  35.1 us
    unnamed x60, local copies, waits for them, and re-layouts  20 us
    dot_general x4, matrix products, body(): jnp.einsum('roij,rojp->rip', full_tiles, windows, preferred_element_type=...  17.6 us
    ppermute x4, waiting for transfers between devices, extended(): before = lax.ppermute(last, axis, up)  16.5 us
    ppermute x4, starting transfers between devices, extended(): after = lax.ppermute(initial, axis, down)  7.37 us
  transfers between devices with their start and end apart: 9, of which 6 were waited for; matrix products, arithmetic and copies ran while one was open for 5% of the time, Pallas kernels for 0%

profile of v1, /device:TPU:0, one launch (start us, length us, event | category | flops | bytes accessed | tf_op | source)
XLA Modules:
  0.0 245.3 jit_solution(14478912724140268293)
XLA Ops:
  8.4 2.9 %collective-permute-start.1 = (bf16[1024,128]{1,0:T(8,128)(2,1)}, bf16[1024,128]{1,0:T(8,128)(2,1)S(1)}, u32[]{:S(2)}, u32[]{:S(2)}) collective-permute-start(bf16[1024,128]{1,0:T(8,128)(2,1)} %param.9), channel_id=1, source_target_pairs={{4,0},{8,4},{12,8},{16,12},{20,16},{24,20},{28,24},{0,28},{5,1},{9... | collective-permute-start | bytes 786440 | tf_op jit(solution)/shard_map/ppermute | solution.py:19
  13.2 2.5 %collective-permute-done = bf16[1024,128]{1,0:T(8,128)(2,1)S(1)} collective-permute-done((bf16[1024,128]{1,0:T(8,128)(2,1)}, bf16[1024,128]{1,0:T(8,128)(2,1)S(1)}, u32[]{:S(2)}, u32[]{:S(2)}) %collective-permute-start) | collective-permute-done | bytes 262176 | tf_op jit(solution)/shard_map/ppermute | solution.py:18
  15.8 1.5 collective-permute-done.1
  25.3 76.5 %all-gather.10.cloned.1.call-done = bf16[4,9,256,256]{3,2,1,0:T(8,128)(2,1)} async-done(((bf16[4,9,64,256]{3,2,1,0:T(8,128)(2,1)}), bf16[4,9,256,256]{3,2,1,0:T(8,128)(2,1)}) %all-gather.10.cloned.1.call-update) | async-done | bytes 4718608 | tf_op jit(solution)/shard_map/all_gather | solution.py:33
  101.7 4.0 %fusion.41 = f32[4,256,128]{1,2,0:T(8,128)S(1)} fusion(bf16[4,9,256,256]{3,2,1,0:T(8,128)(2,1)} %all-gather.10.cloned.1.call-done, bf16[4,9,256,128]{2,3,1,0:T(8,128)(2,1)S(1)} %constant_dynamic-update-slice_fusion.4, bf16[4,9]{1,0:T(4,128)(2,1)S(1)} %convert_element_type.38), kind=kOutput, calls=%fused_computation.19 | convolution fusion | flops 605290496 | bytes 7602248 | tf_op jit(solution)/shard_map/roij,rojp->rip/dot_general | solution.py:45
  107.0 2.6 %collective-permute-start.3 = (bf16[1024,128]{1,0:T(8,128)(2,1)S(1)}, bf16[1024,128]{1,0:T(8,128)(2,1)S(1)}, u32[]{:S(2)}, u32[]{:S(2)}) collective-permute-start(bf16[1024,128]{1,0:T(8,128)(2,1)S(1)} %fusion.53), channel_id=1, source_target_pairs={{4,0},{8,4},{12,8},{16,12},{20,16},{24,20},{28,24},{0,28},{5,1},{9... | collective-permute-start | bytes 786440 | tf_op jit(solution)/shard_map/ppermute | solution.py:19
  110.6 4.1 %collective-permute-done.2 = bf16[1024,128]{1,0:T(8,128)(2,1)S(1)} collective-permute-done((bf16[1024,128]{1,0:T(8,128)(2,1)S(1)}, bf16[1024,128]{1,0:T(8,128)(2,1)S(1)}, u32[]{:S(2)}, u32[]{:S(2)}) %collective-permute-start.2) | collective-permute-done | bytes 262176 | tf_op jit(solution)/shard_map/ppermute | solution.py:18
  118.4 1.8 copy.96
  120.2 1.8 copy.97
  122.0 1.8 copy.99
  123.7 1.8 copy.100
  131.6 4.0 %fusion.35 = f32[4,256,128]{1,2,0:T(8,128)S(1)} fusion(bf16[4,9,256,256]{3,2,1,0:T(8,128)(2,1)} %all-gather.10.cloned.1.call-done, bf16[4,9,256,128]{2,3,1,0:T(8,128)(2,1)S(1)} %constant_dynamic-update-slice_fusion.13, bf16[4,9]{1,0:T(4,128)(2,1)S(1)} %convert_element_type.38), kind=kOutput, calls=%fused_computation.17 | convolution fusion | flops 605290496 | bytes 7602248 | tf_op jit(solution)/shard_map/roij,rojp->rip/dot_general | solution.py:45
  135.8 1.7 collective-permute-start.4
  139.6 4.7 %collective-permute-done.4 = bf16[1024,128]{1,0:T(8,128)(2,1)S(1)} collective-permute-done((bf16[1024,128]{1,0:T(8,128)(2,1)S(1)}, bf16[1024,128]{1,0:T(8,128)(2,1)S(1)}, u32[]{:S(2)}, u32[]{:S(2)}) %collective-permute-start.4) | collective-permute-done | bytes 262176 | tf_op jit(solution)/shard_map/ppermute | solution.py:18
  147.9 1.8 copy.106
  149.7 1.8 copy.107
  151.5 1.8 copy.109
  153.3 1.8 copy.110
  161.1 4.8 %fusion.29 = f32[4,256,128]{1,2,0:T(8,128)} fusion(bf16[4,9,256,256]{3,2,1,0:T(8,128)(2,1)} %all-gather.10.cloned.1.call-done, bf16[4,9,256,128]{2,3,1,0:T(8,128)(2,1)S(1)} %constant_dynamic-update-slice_fusion.22, bf16[4,9]{1,0:T(4,128)(2,1)S(1)} %convert_element_type.38), kind=kOutput, calls=%fused_computation.15 | convolution fusion | flops 605290496 | bytes 7602248 | tf_op jit(solution)/shard_map/roij,rojp->rip/dot_general | solution.py:45
  167.3 2.0 collective-permute-start.6
  170.8 5.1 %collective-permute-done.6 = bf16[1024,128]{1,0:T(8,128)(2,1)S(1)} collective-permute-done((bf16[1024,128]{1,0:T(8,128)(2,1)S(1)}, bf16[1024,128]{1,0:T(8,128)(2,1)S(1)}, u32[]{:S(2)}, u32[]{:S(2)}) %collective-permute-start.6) | collective-permute-done | bytes 262176 | tf_op jit(solution)/shard_map/ppermute | solution.py:18
  179.8 1.8 copy.116
  181.6 1.8 copy.117
  183.3 1.8 copy.119
  185.1 1.8 copy.120
  186.9 1.8 copy.121
  194.6 4.8 %fusion.23 = f32[4,256,128]{1,2,0:T(8,128)} fusion(bf16[4,9,256,256]{3,2,1,0:T(8,128)(2,1)} %all-gather.10.cloned.1.call-done, bf16[4,9,256,128]{2,3,1,0:T(8,128)(2,1)S(1)} %constant_dynamic-update-slice_fusion.31, bf16[4,9]{1,0:T(4,128)(2,1)S(1)} %convert_element_type.38), kind=kOutput, calls=%fused_computation.13 | convolution fusion | flops 605290496 | bytes 7602248 | tf_op jit(solution)/shard_map/roij,rojp->rip/dot_general | solution.py:45
  200.6 2.0 fusion.49
  202.7 11.1 %all-gather.7 = f32[8,1,128]{2,1,0:T(1,128)S(1)} all-gather(f32[1,1,128]{2,1,0:T(1,128)S(1)} %bitcast.140), channel_id=5, replica_groups=mesh['orb'=8,'probe'=4] {'orb'}, dimensions={0}, use_global_device_ids=true | all-gather | bytes 4608 | tf_op jit(solution)/shard_map/all_gather | solution.py:51
  213.8 7.5 %all-gather.6 = f32[8,1,128]{2,1,0:T(1,128)S(1)} all-gather(f32[1,1,128]{2,1,0:T(1,128)S(1)} %bitcast.139), channel_id=4, replica_groups=mesh['orb'=8,'probe'=4] {'orb'}, dimensions={0}, use_global_device_ids=true | all-gather | bytes 4608 | tf_op jit(solution)/shard_map/all_gather | solution.py:51
  221.3 9.0 %all-gather.5 = f32[8,1,128]{2,1,0:T(1,128)S(1)} all-gather(f32[1,1,128]{2,1,0:T(1,128)S(1)} %bitcast.138), channel_id=3, replica_groups=mesh['orb'=8,'probe'=4] {'orb'}, dimensions={0}, use_global_device_ids=true | all-gather | bytes 4608 | tf_op jit(solution)/shard_map/all_gather | solution.py:51
  230.3 7.5 %all-gather.4 = f32[8,1,128]{2,1,0:T(1,128)S(1)} all-gather(f32[1,1,128]{2,1,0:T(1,128)S(1)} %bitcast.137), channel_id=2, replica_groups=mesh['orb'=8,'probe'=4] {'orb'}, dimensions={0}, use_global_device_ids=true | all-gather | bytes 4608 | tf_op jit(solution)/shard_map/all_gather | solution.py:51
  (118 shorter events, 49.1 us)
Async XLA Ops:
  7.2 8.6 %copy-start.1 = (bf16[1024,128]{1,0:T(8,128)(2,1)S(1)}, bf16[1024,128]{1,0:T(8,128)(2,1)}, u32[]{:S(2)}) copy-start(bf16[1024,128]{1,0:T(8,128)(2,1)} %param.9) | copy-start | bytes 786436
  7.2 94.5 %all-gather.10.cloned.1.call-start = ((), (), s32[]{:S(2)}) async-start(), calls=%async_computation | async-start | bytes 5898240 | tf_op jit(solution)/shard_map/all_gather | solution.py:33
  7.9 7.8 %collective-permute-start = (bf16[1024,128]{1,0:T(8,128)(2,1)}, bf16[1024,128]{1,0:T(8,128)(2,1)S(1)}, u32[]{:S(2)}, u32[]{:S(2)}) collective-permute-start(bf16[1024,128]{1,0:T(8,128)(2,1)} %param.9), channel_id=1, source_target_pairs={{0,4},{4,8},{8,12},{12,16},{16,20},{20,24},{24,28},{28,0},{1,5},{5... | collective-permute-start | bytes 786440 | tf_op jit(solution)/shard_map/ppermute | solution.py:18
  8.4 8.9 %collective-permute-start.1 = (bf16[1024,128]{1,0:T(8,128)(2,1)}, bf16[1024,128]{1,0:T(8,128)(2,1)S(1)}, u32[]{:S(2)}, u32[]{:S(2)}) collective-permute-start(bf16[1024,128]{1,0:T(8,128)(2,1)} %param.9), channel_id=1, source_target_pairs={{4,0},{8,4},{12,8},{16,12},{20,16},{24,20},{28,24},{0,28},{5,1},{9... | collective-permute-start | bytes 786440 | tf_op jit(solution)/shard_map/ppermute | solution.py:19
  23.0 2.1 copy-start.5
  23.0 2.2 copy-start.3
  23.0 2.2 copy-start.4
  23.0 2.2 copy-start.2
  107.0 7.7 %collective-permute-start.2 = (bf16[1024,128]{1,0:T(8,128)(2,1)S(1)}, bf16[1024,128]{1,0:T(8,128)(2,1)S(1)}, u32[]{:S(2)}, u32[]{:S(2)}) collective-permute-start(bf16[1024,128]{1,0:T(8,128)(2,1)S(1)} %fusion.53), channel_id=1, source_target_pairs={{0,4},{4,8},{8,12},{12,16},{16,20},{20,24},{24,28},{28,0},{1,5},{5... | collective-permute-start | bytes 786440 | tf_op jit(solution)/shard_map/ppermute | solution.py:18
  107.0 7.7 %collective-permute-start.3 = (bf16[1024,128]{1,0:T(8,128)(2,1)S(1)}, bf16[1024,128]{1,0:T(8,128)(2,1)S(1)}, u32[]{:S(2)}, u32[]{:S(2)}) collective-permute-start(bf16[1024,128]{1,0:T(8,128)(2,1)S(1)} %fusion.53), channel_id=1, source_target_pairs={{4,0},{8,4},{12,8},{16,12},{20,16},{24,20},{28,24},{0,28},{5,1},{9... | collective-permute-start | bytes 786440 | tf_op jit(solution)/shard_map/ppermute | solution.py:19
  126.5 4.9 %copy-start.7 = (bf16[4,1,256,128]{2,3,1,0:T(8,128)(2,1)S(1)}, bf16[4,1,256,128]{2,3,1,0:T(8,128)(2,1)}, u32[]{:S(2)}) copy-start(bf16[4,1,256,128]{2,3,1,0:T(8,128)(2,1)} %copy.100) | copy-start | bytes 786436
  126.5 5.0 %copy-start.8 = (bf16[4,1,256,128]{2,3,1,0:T(8,128)(2,1)S(1)}, bf16[4,1,256,128]{2,3,1,0:T(8,128)(2,1)}, u32[]{:S(2)}) copy-start(bf16[4,1,256,128]{2,3,1,0:T(8,128)(2,1)} %copy.101) | copy-start | bytes 786436
  135.8 8.4 %collective-permute-start.4 = (bf16[1024,128]{1,0:T(8,128)(2,1)S(1)}, bf16[1024,128]{1,0:T(8,128)(2,1)S(1)}, u32[]{:S(2)}, u32[]{:S(2)}) collective-permute-start(bf16[1024,128]{1,0:T(8,128)(2,1)S(1)} %fusion.52), channel_id=1, source_target_pairs={{0,4},{4,8},{8,12},{12,16},{16,20},{20,24},{24,28},{28,0},{1,5},{5... | collective-permute-start | bytes 786440 | tf_op jit(solution)/shard_map/ppermute | solution.py:18
  137.6 6.7 %collective-permute-start.5 = (bf16[1024,128]{1,0:T(8,128)(2,1)S(1)}, bf16[1024,128]{1,0:T(8,128)(2,1)S(1)}, u32[]{:S(2)}, u32[]{:S(2)}) collective-permute-start(bf16[1024,128]{1,0:T(8,128)(2,1)S(1)} %fusion.52), channel_id=1, source_target_pairs={{4,0},{8,4},{12,8},{16,12},{20,16},{24,20},{28,24},{0,28},{5,1},{9... | collective-permute-start | bytes 786440 | tf_op jit(solution)/shard_map/ppermute | solution.py:19
  156.1 4.9 %copy-start.9 = (bf16[4,1,256,128]{2,3,1,0:T(8,128)(2,1)S(1)}, bf16[4,1,256,128]{2,3,1,0:T(8,128)(2,1)}, u32[]{:S(2)}) copy-start(bf16[4,1,256,128]{2,3,1,0:T(8,128)(2,1)} %copy.110) | copy-start | bytes 786436
  156.1 5.0 %copy-start.10 = (bf16[4,1,256,128]{2,3,1,0:T(8,128)(2,1)S(1)}, bf16[4,1,256,128]{2,3,1,0:T(8,128)(2,1)}, u32[]{:S(2)}) copy-start(bf16[4,1,256,128]{2,3,1,0:T(8,128)(2,1)} %copy.111) | copy-start | bytes 786436
  167.2 33.4 %copy-start = (bf16[1024,128]{1,0:T(8,128)(2,1)}, bf16[1024,128]{1,0:T(8,128)(2,1)S(1)}, u32[]{:S(2)}) copy-start(bf16[1024,128]{1,0:T(8,128)(2,1)S(1)} %fusion.48) | copy-start | bytes 786436
  167.3 8.7 %collective-permute-start.6 = (bf16[1024,128]{1,0:T(8,128)(2,1)S(1)}, bf16[1024,128]{1,0:T(8,128)(2,1)S(1)}, u32[]{:S(2)}, u32[]{:S(2)}) collective-permute-start(bf16[1024,128]{1,0:T(8,128)(2,1)S(1)} %fusion.48), channel_id=1, source_target_pairs={{0,4},{4,8},{8,12},{12,16},{16,20},{20,24},{24,28},{28,0},{1,5},{5... | collective-permute-start | bytes 786440 | tf_op jit(solution)/shard_map/ppermute | solution.py:18
  169.3 6.7 %collective-permute-start.7 = (bf16[1024,128]{1,0:T(8,128)(2,1)S(1)}, bf16[1024,128]{1,0:T(8,128)(2,1)S(1)}, u32[]{:S(2)}, u32[]{:S(2)}) collective-permute-start(bf16[1024,128]{1,0:T(8,128)(2,1)S(1)} %fusion.48), channel_id=1, source_target_pairs={{4,0},{8,4},{12,8},{16,12},{20,16},{24,20},{28,24},{0,28},{5,1},{9... | collective-permute-start | bytes 786440 | tf_op jit(solution)/shard_map/ppermute | solution.py:19
  189.5 4.9 %copy-start.11 = (bf16[4,1,256,128]{2,3,1,0:T(8,128)(2,1)S(1)}, bf16[4,1,256,128]{2,3,1,0:T(8,128)(2,1)}, u32[]{:S(2)}) copy-start(bf16[4,1,256,128]{2,3,1,0:T(8,128)(2,1)} %copy.120) | copy-start | bytes 786436
  189.5 5.0 %copy-start.12 = (bf16[4,1,256,128]{2,3,1,0:T(8,128)(2,1)S(1)}, bf16[4,1,256,128]{2,3,1,0:T(8,128)(2,1)}, u32[]{:S(2)}) copy-start(bf16[4,1,256,128]{2,3,1,0:T(8,128)(2,1)} %copy.121) | copy-start | bytes 786436
  189.5 5.0 %copy-start.6 = (bf16[4,1,256,128]{2,3,1,0:T(8,128)(2,1)S(1)}, bf16[4,1,256,128]{2,3,1,0:T(8,128)(2,1)}, u32[]{:S(2)}) copy-start(bf16[4,1,256,128]{2,3,1,0:T(8,128)(2,1)} %copy.122) | copy-start | bytes 786436
Sparse Core Ops, SparseCore 0:
  9.6 92.0 all-gather.9
